TPU v7x, 128 devices: a whole 4x4x4 slice. The times are simulated.
128 devices in a mesh: seq: 8 (over z, x_lo), res: 16 (over x_hi, y, core).
Axes of the slice: x: 4 (x_hi: 2, x_lo: 2; x = x_hi * 2 + x_lo), y: 4, z: 4, core: 2. Of those that a mesh axis runs over, the one named last changes fastest.
Arguments:
- alignment_rows: bfloat16 [64, 1024, 256], P('seq', 'res'), may hold values from -6 to 6
- pair_entries: bfloat16 [1024, 1024, 128], P('res', 'seq'), may hold values from -6 to 6
- combined_weight: bfloat16 [256, 1024], replicated, may hold values from -0.375 to 0.375
- output_weight: bfloat16 [256, 256], replicated, may hold values from -0.375 to 0.375
- pair_weight: float32 [128, 8], replicated, may hold values from -9 to 9
- updated_gradient: bfloat16 [64, 1024, 256], P('seq', 'res'), may hold values from -6 to 6
Outputs:
- updated: bfloat16 [64, 1024, 256], P('seq', 'res')
- alignment_gradient: bfloat16 [64, 1024, 256], P('seq', 'res')
- pair_gradient: bfloat16 [1024, 1024, 128], P('res', 'seq')
- combined_weight_gradient: float32 [256, 1024], replicated
- output_weight_gradient: float32 [256, 256], replicated
- pair_weight_gradient: float32 [128, 8], replicated
All inputs are finite; a program needn't handle non-finite values.
Results may differ from a plain program's by a relative error of at most 0.011.
Values may be sent and summed in bfloat16 or wider, within the bound.
A program may use at most 128 MiB of HBM per device.

v0:
```python
import math

import jax
import jax.numpy as jnp
from jax import lax
from jax.sharding import PartitionSpec as P

eps_norm = 1e-05


def layer_normalize(values):
    values = values.astype(jnp.float32)
    center = values - jnp.mean(values, axis=-1, keepdims=True)
    broadcast_pair = lax.rsqrt(jnp.mean(center * center, axis=-1, keepdims=True) + eps_norm)
    return (center * broadcast_pair, broadcast_pair)


def layer_norm_backward(normalized_gradient, normalized_rows, broadcast_pair):
    mean_grad = jnp.mean(normalized_gradient, axis=-1, keepdims=True)
    mean_cross = jnp.mean(normalized_gradient * normalized_rows, axis=-1, keepdims=True)
    return broadcast_pair * (normalized_gradient - mean_grad - normalized_rows * mean_cross)


def split_heads(tensor, head_count):
    return tensor.reshape(
        tensor.shape[0], tensor.shape[1], head_count, tensor.shape[2] // head_count
    )


def merge_heads(tensor):
    return tensor.reshape(tensor.shape[0], tensor.shape[1], tensor.shape[2] * tensor.shape[3])


def body(
    alignment_rows, pair_entries, combined_weight, output_weight, pair_weight, updated_gradient
):
    sequence_count, residue_count, alignment_width = alignment_rows.shape
    head_count = pair_weight.shape[1]
    query_width = output_weight.shape[0]
    head_dim = query_width // head_count
    column_count = pair_entries.shape[1]
    token_count = sequence_count * residue_count
    score_scale = 1.0 / math.sqrt(head_dim * sequence_count * lax.axis_size("seq"))
    normalized_rows, broadcast_pair = layer_normalize(alignment_rows)
    normalized_rows_backward = normalized_rows.astype(jnp.bfloat16).reshape(
        token_count, alignment_width
    )
    projected = jnp.dot(
        normalized_rows_backward, combined_weight, preferred_element_type=jnp.float32
    ).reshape(sequence_count, residue_count, 4 * query_width)
    queries = (projected[..., :query_width] * score_scale).astype(jnp.bfloat16)
    key_rows = projected[..., query_width : 2 * query_width].astype(jnp.bfloat16)
    value_rows = projected[..., 2 * query_width : 3 * query_width].astype(jnp.bfloat16)
    gate_open = jax.nn.sigmoid(projected[..., 3 * query_width :])
    all_keys, all_values = (
        lax.all_gather(key_rows, "res", axis=1, tiled=True),
        lax.all_gather(value_rows, "res", axis=1, tiled=True),
    )
    query_heads = split_heads(queries, head_count)
    key_heads = split_heads(all_keys, head_count)
    value_heads = split_heads(all_values, head_count)
    score_terms = jnp.einsum(
        "sihd,sjhd->hij", query_heads, key_heads, preferred_element_type=jnp.float32
    )
    pair_normed, pair_spread = layer_normalize(pair_entries)
    pair_bias = jnp.einsum("ijc,ch->hij", pair_normed, pair_weight, precision=lax.Precision.HIGHEST)
    col_start = lax.axis_index("seq") * column_count
    own_block = lax.dynamic_slice_in_dim(score_terms, col_start, column_count, 2) + pair_bias
    logits = lax.psum(lax.dynamic_update_slice_in_dim(score_terms, own_block, col_start, 2), "seq")
    row_top = jnp.max(logits, axis=-1, keepdims=True)
    lifted = jnp.exp(logits - row_top)
    softmax_out = lifted / jnp.sum(lifted, axis=-1, keepdims=True)
    softmax_low = softmax_out.astype(jnp.bfloat16)
    attended = merge_heads(
        jnp.einsum("hij,sjhd->sihd", softmax_low, value_heads, preferred_element_type=jnp.float32)
    )
    gated_out = (gate_open * attended).astype(jnp.bfloat16)
    flattened_gated = gated_out.reshape(token_count, query_width)
    updated = (
        jnp.dot(flattened_gated, output_weight, preferred_element_type=jnp.float32)
        .astype(jnp.bfloat16)
        .reshape(sequence_count, residue_count, alignment_width)
    )
    flattened_gradient = updated_gradient.reshape(token_count, alignment_width)
    grad_gated = jnp.dot(
        flattened_gradient, output_weight.T, preferred_element_type=jnp.float32
    ).reshape(sequence_count, residue_count, query_width)
    out_local = jnp.dot(flattened_gated.T, flattened_gradient, preferred_element_type=jnp.float32)
    grad_attended = (grad_gated * gate_open).astype(jnp.bfloat16)
    grad_gate_logit = grad_gated * attended * gate_open * (1.0 - gate_open)
    attended_grad_heads = split_heads(grad_attended, head_count)
    grad_terms = jnp.einsum(
        "sihd,sjhd->hij", attended_grad_heads, value_heads, preferred_element_type=jnp.float32
    )
    grad_probs = lax.psum(grad_terms, "seq")
    row_dot = jnp.sum(softmax_out * grad_probs, axis=-1, keepdims=True)
    grad_logits = softmax_out * (grad_probs - row_dot)
    grad_logits_b = grad_logits.astype(jnp.bfloat16)
    logit_share = lax.dynamic_slice_in_dim(grad_logits, col_start, column_count, 2)
    grad_query_heads = (
        jnp.einsum("hij,sjhd->sihd", grad_logits_b, key_heads, preferred_element_type=jnp.float32)
        * score_scale
    )
    key_part = jnp.einsum(
        "hij,sihd->jshd", grad_logits_b, query_heads, preferred_element_type=jnp.float32
    )
    value_part = jnp.einsum(
        "hij,sihd->jshd", softmax_low, attended_grad_heads, preferred_element_type=jnp.float32
    )
    summed = lax.psum_scatter(
        jnp.concatenate([merge_heads(key_part), merge_heads(value_part)], axis=-1),
        "res",
        scatter_dimension=0,
        tiled=True,
    )
    key_value_grads = jnp.transpose(summed, (1, 0, 2))
    projected_gradient = jnp.concatenate(
        [merge_heads(grad_query_heads), key_value_grads, grad_gate_logit], axis=-1
    )
    projected_gradient = projected_gradient.astype(jnp.bfloat16).reshape(
        token_count, 4 * query_width
    )
    qkvg_local = jnp.dot(
        normalized_rows_backward.T, projected_gradient, preferred_element_type=jnp.float32
    )
    normalized_gradient = jnp.dot(
        projected_gradient, combined_weight.T, preferred_element_type=jnp.float32
    ).reshape(sequence_count, residue_count, alignment_width)
    alignment_gradient = layer_norm_backward(
        normalized_gradient, normalized_rows, broadcast_pair
    ).astype(jnp.bfloat16)
    pair_w_local = jnp.einsum(
        "ijc,hij->ch", pair_normed, logit_share, precision=lax.Precision.HIGHEST
    )
    grad_pair_normed = jnp.einsum(
        "hij,ch->ijc", logit_share, pair_weight, precision=lax.Precision.HIGHEST
    )
    pair_gradient = layer_norm_backward(grad_pair_normed, pair_normed, pair_spread).astype(
        jnp.bfloat16
    )
    combined_weight_gradient, output_weight_gradient, pair_weight_gradient = lax.psum(
        (qkvg_local, out_local, pair_w_local), ("seq", "res")
    )
    return (
        updated,
        alignment_gradient,
        pair_gradient,
        combined_weight_gradient,
        output_weight_gradient,
        pair_weight_gradient,
    )


def solution(mesh):
    return jax.shard_map(
        body,
        mesh=mesh,
        in_specs=(
            P("seq", "res", None),
            P("res", "seq", None),
            P(),
            P(),
            P(),
            P("seq", "res", None),
        ),
        out_specs=(
            P("seq", "res", None),
            P("seq", "res", None),
            P("res", "seq", None),
            P(),
            P(),
            P(),
        ),
        check_vma=False,
    )
```

profile of v0, /device:TPU:1, one launch (start us, length us, event | category | flops | bytes accessed | tf_op | source)
XLA Modules:
  0.0 690.6 jit_solution(11635199997890458945)
XLA Ops:
  9.6 2.8 fusion.80
  14.1 3.3 copy.33
  17.4 2.4 multiply_convert_fusion.1
  22.4 2.6 fusion.7
  25.0 47.2 %all-gather.5.cloned.1.call-done = bf16[8,1024,256]{2,1,0:T(8,128)(2,1)} async-done(((bf16[8,64,256]{2,1,0:T(8,128)(2,1)}), bf16[8,1024,256]{2,1,0:T(8,128)(2,1)}) %all-gather.5.cloned.1.call-update) | async-done | bytes 4194320 | tf_op jit(solution)/shard_map/all_gather | solution.py:56
  72.2 6.5 copy.30
  78.7 4.4 convolution_bitcast_fusion.3
  83.1 45.3 %all-gather.3.cloned.1.call-done = bf16[8,1024,256]{2,1,0:T(8,128)(2,1)} async-done(((bf16[8,64,256]{2,1,0:T(8,128)(2,1)}), bf16[8,1024,256]{2,1,0:T(8,128)(2,1)}) %all-gather.3.cloned.1.call-update) | async-done | bytes 4194320 | tf_op jit(solution)/shard_map/all_gather | solution.py:57
  128.4 6.4 copy.28
  134.9 4.6 convolution_bitcast_fusion.2
  141.4 180.9 %all-reduce.7.cloned.1.call-done = (f32[8,64,1024]{2,1,0:T(8,128)}, f32[8,64,1024]{2,1,0:T(8,128)}) async-done(((f32[8,64,1024]{2,1,0:T(8,128)}, f32[8,64,1024]{2,1,0:T(8,128)}), (f32[8,64,1024]{2,1,0:T(8,128)}, f32[8,64,1024]{2,1,0:T(8,128)})) %all-reduce.7.cloned.1.call-update) | async-done | bytes 4194320 | tf_op jit(solution)/shard_map/psum | solution.py:69
  322.3 3.9 fusion.81
  326.2 7.0 %convolution_bitcast_fusion = f32[1024,8,8,32]{0,3,1,2:T(8,128)} fusion(bf16[8,64,8,32]{1,3,2,0:T(8,128)(2,1)} %bitcast.92, f32[8,64]{1,0:T(8,128)S(1)} %get-tuple-element.35, f32[8,64,1024]{2,1,0:T(8,128)} %get-tuple-element.24), kind=kOutput, calls=%fused_computation.19 | convolution fusion | flops 270009856 | bytes 10749952 | tf_op jit(solution)/shard_map/hij,sihd->jshd/dot_general | solution.py:107
  333.2 2.7 multiply_reduce_fusion
  336.1 4.0 subtract_multiply_fusion
  340.1 4.1 copy.47
  344.2 9.1 %copy.49 = f32[1024,8,256]{2,0,1:T(8,128)} copy(f32[1024,8,256]{0,2,1:T(8,128)} %bitcast.81) | data formatting | bytes 16777216 | tf_op jit(solution)/shard_map/reshape | solution.py:31
  353.3 2.8 convolution_bitcast_fusion.1
  356.1 4.1 copy.45
  360.2 9.1 %copy.48 = f32[1024,8,256]{2,0,1:T(8,128)} copy(f32[1024,8,256]{0,2,1:T(8,128)} %bitcast.82) | data formatting | bytes 16777216 | tf_op jit(solution)/shard_map/reshape | solution.py:31
  369.3 11.8 %pad_maximum_fusion = f32[1024,8,512]{2,0,1:T(8,128)} fusion(f32[1024,8,256]{2,0,1:T(8,128)} %copy.49, f32[1024,8,256]{2,0,1:T(8,128)} %copy.48), kind=kLoop, calls=%fused_computation.1 | loop fusion | flops 4194304 | bytes 33554432 | tf_op jit(solution)/shard_map/concatenate | solution.py:111
  381.4 5.8 fusion.22
  387.2 2.3 copy.37
  391.2 5.3 fusion.31
  400.3 4.2 fusion.77
  404.5 2.8 fusion.12
  407.3 4.3 copy.55
  411.6 3.6 fusion.34
  415.2 82.3 %psum.39 = f32[128,8]{0,1:T(8,128)} all-reduce(f32[128,8]{0,1:T(8,128)S(1)} %fusion.34), channel_id=1, replica_groups=mesh['seq'=8,'res'=16] {'seq','res'}, use_global_device_ids=true, to_apply=%region_16.0 | all-reduce | flops 1024 | bytes 8192 | tf_op jit(solution)/shard_map/psum | solution.py:141
  500.9 28.0 %reduce-scatter.2.cloned.1.call-done = f32[64,8,512]{2,0,1:T(8,128)} async-done(((f32[1024,8,512]{2,0,1:T(8,128)}), f32[64,8,512]{2,0,1:T(8,128)}) %reduce-scatter.2.cloned.1.call-update) | async-done | bytes 1048592 | tf_op jit(solution)/shard_map/reduce_scatter | solution.py:110
  533.5 147.5 %all-reduce.5.cloned.1.call-done = (f32[256,1024]{1,0:T(8,128)}, f32[256,256]{1,0:T(8,128)}) async-done(((f32[256,1024]{1,0:T(8,128)}, f32[256,256]{1,0:T(8,128)}), (f32[256,1024]{1,0:T(8,128)}, f32[256,256]{1,0:T(8,128)})) %all-reduce.5.cloned.1.call-update) | async-done | bytes 1310736 | tf_op jit(solution)/shard_map/psum | solution.py:141
  681.0 2.3 copy.92
  (56 shorter events, 23.0 us)
Async XLA Ops:
  7.2 2.5 copy-start
  7.2 65.1 %all-gather.5.cloned.1.call-start = ((), (), s32[]{:S(2)}) async-start(), calls=%async_computation.2 | async-start | bytes 4456448 | tf_op jit(solution)/shard_map/all_gather | solution.py:56
  13.3 115.1 %all-gather.3.cloned.1.call-start = ((), (), s32[]{:S(2)}) async-start(), calls=%async_computation.1 | async-start | bytes 4456448 | tf_op jit(solution)/shard_map/all_gather | solution.py:57
  14.0 308.3 %all-reduce.7.cloned.1.call-start = ((), (), s32[]{:S(2)}) async-start(), calls=%async_computation.5 | async-start | bytes 8388608 | tf_op jit(solution)/shard_map/psum | solution.py:69
  14.1 3.3 copy-start.6
  21.1 1.3 copy-start.8
  141.2 387.7 %reduce-scatter.2.cloned.1.call-start = ((), (), s32[]{:S(2)}) async-start(), calls=%async_computation.3 | async-start | bytes 17825792 | tf_op jit(solution)/shard_map/reduce_scatter | solution.py:110
  333.2 2.9 copy-start.1
  333.2 6.9 copy-start.2
  381.2 299.9 %all-reduce.5.cloned.1.call-start = ((), (), s32[]{:S(2)}) async-start(), calls=%async_computation.4 | async-start | bytes 2621440 | tf_op jit(solution)/shard_map/psum | solution.py:141
  415.2 83.8 %copy-start.9 = (bf16[8,64,256]{2,1,0:T(8,128)(2,1)S(1)}, bf16[8,64,256]{2,1,0:T(8,128)(2,1)}, u32[]{:S(2)}) copy-start(bf16[8,64,256]{2,1,0:T(8,128)(2,1)} %param.11) | copy-start | bytes 786436
  415.2 84.8 %copy-start.7 = (bf16[256,256]{1,0:T(8,128)(2,1)S(1)}, bf16[256,256]{1,0:T(8,128)(2,1)}, u32[]{:S(2)}) copy-start(bf16[256,256]{1,0:T(8,128)(2,1)} %param.9) | copy-start | bytes 393220
  497.5 32.7 %copy-start.3 = (bf16[8,64,256]{2,1,0:T(8,128)(2,1)S(1)}, bf16[8,64,256]{2,1,0:T(8,128)(2,1)}, u32[]{:S(2)}) copy-start(bf16[8,64,256]{2,1,0:T(8,128)(2,1)} %param.6) | copy-start | bytes 786436
  497.5 32.7 %copy-start.4 = (bf16[8,64,256]{2,1,0:T(8,128)(2,1)S(1)}, bf16[8,64,256]{2,1,0:T(8,128)(2,1)}, u32[]{:S(2)}) copy-start(bf16[8,64,256]{2,1,0:T(8,128)(2,1)} %copy.51) | copy-start | bytes 786436
  681.0 2.4 copy-start.5
Sparse Core Ops, SparseCore 0:
  13.4 58.7 all-gather.4
  75.3 53.0 all-gather.2
  141.3 180.9 all-reduce.6
  381.3 147.6 reduce-scatter.1
  534.3 146.6 all-reduce.4
where the time goes:
time: 692 us; the launch traced here: 691 us
  waiting for transfers between devices  450 us (65%)
  blocking collectives  82.3 us (12%)
  local copies, waits for them, and re-layouts  59.9 us (9%)
  matrix products  49.5 us (7%)
  other arithmetic  34.5 us (5%)
  between operations  14 us (2%)
    psum x1, waiting for transfers between devices, body(): lax.psum(lax.dynamic_update_slice_in_dim(score_terms, own_block, col_star...  181 us
    psum x1, waiting for transfers between devices, body(): lax.psum((qkvg_local, out_local, pair_w_local), ('seq', 'res'))  148 us
    psum x1, blocking collectives, body(): lax.psum((qkvg_local, out_local, pair_w_local), ('seq', 'res'))  82.3 us
    all_gather x1, waiting for transfers between devices, body(): lax.all_gather(key_rows, 'res', axis=1, tiled=True)  47.2 us
    all_gather x1, waiting for transfers between devices, body(): lax.all_gather(value_rows, 'res', axis=1, tiled=True)  45.3 us
    reduce_scatter x1, waiting for transfers between devices, body(): lax.psum_scatter(jnp.concatenate([merge_heads(key_part), merge_heads(valu...  28 us
    reshape x3, local copies, waits for them, and re-layouts, merge_heads(): tensor.reshape(tensor.shape[0], tensor.shape[1], tensor.shape[2] * tensor...  19.9 us
  transfers between devices with their start and end apart: 5, of which 5 were waited for; matrix products, arithmetic and copies ran while one was open for 9% of the time, Pallas kernels for 0%

commit v1 on v0

v1 whole, which is shorter than its diff:
```python
import math

import jax
import jax.numpy as jnp
from jax import lax
from jax.experimental import pallas as pl
from jax.experimental.pallas import tpu as pltpu
from jax.sharding import PartitionSpec as P

MESH = pl.DeviceIdType.MESH
EPS = 1e-05
SCALE = 1.0 / math.sqrt(2048)
F32 = jnp.float32
BF16 = jnp.bfloat16

IN_QA, IN_KV, GY, GX, GS, GF = 0, 8, 16, 48, 56, 64
PB_A, PB_Y, STAT = 72, 80, 84
OY, OS, OX, RT_A, RT_K = 88, 120, 128, 136, 144
DL_Y, DL_A = 152, 156
T_C, T_S, T_X, T_Y, T_AS, T_AC = 164, 165, 173, 174, 178, 186
SEM_COUNT = 187


def nt(a, b):
    return lax.dot_general(a, b, (((1,), (1,)), ((), ())), preferred_element_type=F32)


def tn(a, b):
    return lax.dot_general(a, b, (((0,), (0,)), ((), ())), preferred_element_type=F32)


def nn(a, b):
    return jnp.dot(a, b, preferred_element_type=F32)


def split2(v):
    hi = v.astype(BF16)
    lo = (v - hi.astype(F32)).astype(BF16)
    return hi, lo


def split3(v):
    hi = v.astype(BF16)
    rest = v - hi.astype(F32)
    mid = rest.astype(BF16)
    lo = (rest - mid.astype(F32)).astype(BF16)
    return hi, mid, lo


def kernel(
    al, pe, cw, ow, pwt, ug,
    upd, alg, pg, dcw, dow, dpw,
    nf, spb, nb, nbt, gate, gg, heads4, sb, qa, kv,
    xn, rst, bs, pb, bi, bt, st, lt, dpt, oa, okv, ra, rsb, xb, rx, rb, ret,
    dl, dr, dx, dpj, ch, chr_, ch2, chs, chx, chy, chf, pwacc,
    ssem, rsem,
):
    s = lax.axis_index("seq")
    r = lax.axis_index("res")
    z, xl = s // 2, s % 2
    xh, y, c = r // 8, (r // 2) % 4, r % 2
    p = xh * 2 + c

    def at_seq(k):
        return {"seq": ((z + k // 2) % 4) * 2 + (xl + k) % 2}

    def from_seq(k):
        return {"seq": ((z + 4 - k // 2) % 4) * 2 + (xl + k) % 2}

    def at_y(d):
        return {"res": xh * 8 + ((y + d) % 4) * 2 + c}

    at_x = {"res": (1 - xh) * 8 + y * 2 + c}
    at_c = {"res": xh * 8 + y * 2 + (1 - c)}

    def send(src, dst, i, where):
        return pltpu.make_async_remote_copy(
            src_ref=src, dst_ref=dst, send_sem=ssem.at[i], recv_sem=rsem.at[i],
            device_id=where, device_id_type=MESH,
        )

    bar = pltpu.get_barrier_semaphore()
    for k in range(1, 8):
        pl.semaphore_signal(bar, inc=1, device_id=at_seq(k), device_id_type=MESH)
    for d in range(1, 4):
        pl.semaphore_signal(bar, inc=1, device_id=at_y(d), device_id_type=MESH)
    pl.semaphore_signal(bar, inc=1, device_id=at_x, device_id_type=MESH)
    pl.semaphore_signal(bar, inc=1, device_id=at_c, device_id_type=MESH)

    def c_in_qa(k):
        return send(sb.at[at_seq(k)["seq"], pl.ds(0, 2)], qa.at[k, y], IN_QA + k, at_seq(k))

    def c_in_kv(k):
        return send(sb.at[at_seq(k)["seq"], pl.ds(2, 2)], kv.at[k, p], IN_KV + k, at_seq(k))

    def c_gy(k, d):
        return send(qa.at[k, y], qa.at[k, y], GY + k * 4 + d, at_y(d))

    def c_gx(k):
        return send(kv.at[k, p], kv.at[k, p], GX + k, at_x)

    def c_gs(k):
        return send(kv.at[k, p], kv.at[k, p], GS + k, at_c)

    px = (1 - xh) * 2 + c

    def c_gf(k):
        return send(kv.at[k, px], kv.at[k, px], GF + k, at_c)

    def c_pa(k):
        return send(bs.at[at_seq(k)["seq"]], pb.at[s // 4, s % 4], PB_A + k, at_seq(k))

    def c_py(d):
        return send(pb.at[:, (y + d) % 4], bi.at[y], PB_Y + d, at_y(d))

    def c_st(d):
        return send(st.at[y], st.at[y], STAT + d, at_y(d))

    def c_oy(k, d):
        return send(oa.at[k, (y + d) % 4], ra.at[k, d], OY + k * 4 + d, at_y(d))

    def c_os(k):
        return send(okv.at[k, 1 - c], rsb.at[k], OS + k, at_c)

    def c_ox(k):
        return send(xb.at[k], rx.at[k], OX + k, at_x)

    def c_ra(k):
        return send(rb.at[k, pl.ds(0, 2)], ret.at[s, pl.ds(0, 2)], RT_A + k, from_seq(k))

    def c_rk(k):
        return send(rb.at[k, pl.ds(2, 2)], ret.at[s, pl.ds(2, 2)], RT_K + k, from_seq(k))

    def c_dy(d):
        return send(dl.at[(y + d) % 4], dr.at[:, y], DL_Y + d, at_y(d))

    def c_da(k):
        w = at_seq(k)["seq"]
        return send(dr.at[w // 4, w % 4], dx.at[s], DL_A + k, at_seq(k))

    def c_tc():
        return send(ch.at[1 - c], chr_, T_C, at_c)

    def c_ts(k):
        return send(ch2.at[at_seq(k)["seq"]], chs.at[k], T_S + k, at_seq(k))

    def c_tx():
        return send(chs.at[0], chx.at[0], T_X, at_x)

    def c_ty(d):
        return send(chx.at[1], chy.at[d], T_Y + d, at_y(d))

    def c_as(k):
        return send(chf.at[c, s], chf.at[c, s], T_AS + k, at_seq(k))

    def c_ac():
        return send(chf.at[c], chf.at[c], T_AC, at_c)

    for q in range(8):
        x = al[q].astype(F32)
        cen = x - jnp.mean(x, axis=-1, keepdims=True)
        spread = lax.rsqrt(jnp.mean(cen * cen, axis=-1, keepdims=True) + EPS)
        normed = cen * spread
        rows = pl.ds(q * 64, 64)
        nf[rows, :] = normed
        spb[rows, :] = jnp.broadcast_to(spread, (64, 128))
        nb[rows, :] = normed.astype(BF16)
    for q in range(8):
        rows = pl.ds(q * 64, 64)
        n = nb[rows, :]
        heads4[0, q] = (nn(n, cw[:, 0:256]) * SCALE).astype(BF16)
        heads4[2, q] = nn(n, cw[:, 256:512]).astype(BF16)
        heads4[3, q] = nn(n, cw[:, 512:768]).astype(BF16)
        open_ = 1.0 / (1.0 + jnp.exp(-nn(n, cw[:, 768:1024])))
        gate[rows, :] = open_
        grad = nt(ug[q], ow[...])
        gg[rows, :] = grad
        heads4[1, q] = (grad * open_).astype(BF16)
    for h in range(8):
        for t in range(4):
            sb[h, t] = jnp.concatenate(
                [heads4[t, q][:, h * 32:(h + 1) * 32] for q in range(8)], axis=-1
            )

    pl.semaphore_wait(bar, 12)

    def start_in(k, _):
        c_in_qa(k).start()
        c_in_kv(k).start()
        return 0

    lax.fori_loop(1, 8, start_in, 0)
    qa[0, y] = sb[s, 0:2]
    kv[0, p] = sb[s, 2:4]

    def forward(k):
        for d in (1, 3, 2):
            c_gy(k, d).start()
        c_gx(k).start()
        c_gs(k).start()

    ones = jnp.ones((128, 128), BF16)
    w_all = pwt[...]
    w3 = jnp.concatenate(split3(w_all), axis=0)

    def pair_chunk(k):
        base = pl.multiple_of(k * 1024, 1024)
        x = pe[pl.ds(k * 8, 8)].reshape(1024, 128)
        cen = x.astype(F32) - nn(x, ones) * (1.0 / 128)
        hi, lo = split2(cen * cen)
        spread = lax.rsqrt((nn(hi, ones) + nn(lo, ones)) * (1.0 / 128) + EPS)
        normed = cen * spread
        xn[pl.ds(base, 1024), :] = normed
        rst[pl.ds(base, 1024), :] = spread
        hi, lo = split2(normed)
        b = nt(w3, hi) + nt(w3, lo)
        b = b[0:8] + b[8:16] + b[16:24]
        for q in range(8):
            bs[:, k * 8 + q, :] = b[:, q * 128:(q + 1) * 128]

    forward(0)
    pair_chunk(0)

    def stage_in(k, _):
        c_in_qa(k).wait_recv()
        c_in_kv(k).wait_recv()
        forward(k)
        c_gx(k - 1).wait_recv()
        c_gf(k - 1).start()
        pair_chunk(k)
        return 0

    lax.fori_loop(1, 8, stage_in, 0)
    c_gx(7).wait_recv()
    c_gf(7).start()

    def start_pair(k, _):
        c_pa(k).start()
        return 0

    lax.fori_loop(1, 8, start_pair, 0)
    pb[s // 4, s % 4] = bs[s]
    nbt[...] = nb[...].T

    def wait_pair(k, _):
        c_pa(k).wait_recv()
        return 0

    lax.fori_loop(1, 8, wait_pair, 0)
    for d in range(1, 4):
        c_py(d).start()
    bi[y] = pb[:, y]

    lt[...] = jnp.zeros_like(lt)
    dpt[...] = jnp.zeros_like(dpt)

    def stage_mm(k, _):
        for d in range(1, 4):
            c_gy(k, d).wait_recv()
        c_gs(k).wait_recv()
        c_gf(k).wait_recv()
        qk = qa[k, :, 0].reshape(256, 256)
        dak = qa[k, :, 1].reshape(256, 256)
        kk = kv[k, :, 0].reshape(256, 256)
        vk = kv[k, :, 1].reshape(256, 256)
        lt[...] += nt(kk, qk)
        dpt[...] += nt(vk, dak)
        return 0

    lax.fori_loop(0, 8, stage_mm, 0)
    for d in range(1, 4):
        c_py(d).wait_recv()
    bias = jnp.concatenate(
        [jnp.concatenate([bi[a, b] for a in range(4)], axis=0) for b in range(2)], axis=1
    )
    logits = lt[...] + bias.T
    top = jnp.max(logits, axis=0, keepdims=True)
    e = jnp.exp(logits - top)
    dp = dpt[...]
    total = jnp.sum(e, axis=0, keepdims=True)
    dots = jnp.sum(e * dp, axis=0, keepdims=True)
    st[y] = jnp.concatenate([top, total, dots, jnp.zeros((5, 256), F32)], axis=0)
    for d in range(1, 4):
        c_st(d).start()
    lt[...] = e
    for d in range(1, 4):
        c_st(d).wait_recv()
    stats = [st[a] for a in range(4)]
    peak = jnp.maximum(
        jnp.maximum(stats[0][0:1], stats[1][0:1]), jnp.maximum(stats[2][0:1], stats[3][0:1])
    )
    z_sum = jnp.zeros((1, 256), F32)
    d_sum = jnp.zeros((1, 256), F32)
    for a in range(4):
        f = jnp.exp(stats[a][0:1] - peak)
        z_sum += f * stats[a][1:2]
        d_sum += f * stats[a][2:3]
    inv = 1.0 / z_sum
    mine = st[y]
    prob_t = lt[...] * (jnp.exp(mine[0:1] - peak) * inv)
    grad_t = prob_t * (dpt[...] - d_sum * inv)
    lt[...] = prob_t
    dpt[...] = grad_t
    grad = grad_t.T
    for a in range(4):
        for b in range(2):
            dl[a, b] = grad[a * 64:(a + 1) * 64, b * 128:(b + 1) * 128]
    for d in range(1, 4):
        c_dy(d).start()
    dr[:, y] = dl[y]
    bt[0] = lt[...].astype(BF16)
    bt[1] = bt[0].T
    bt[2] = dpt[...].astype(BF16)
    bt[3] = grad.astype(BF16)

    def stage_out(k):
        qk = qa[k, :, 0].reshape(256, 256)
        dak = qa[k, :, 1].reshape(256, 256)
        kk = kv[k, :, 0].reshape(256, 256)
        vk = kv[k, :, 1].reshape(256, 256)
        oa[k, :, 0] = nn(bt[1], vk).astype(BF16).reshape(4, 64, 256)
        oa[k, :, 1] = (nn(bt[3], kk) * SCALE).astype(BF16).reshape(4, 64, 256)
        for d in (1, 3, 2):
            c_oy(k, d).start()
        dk = nn(bt[2], qk).astype(BF16)
        dv = nn(bt[0], dak).astype(BF16)
        for a in range(2):
            for b in range(2):
                at = (a * 2 + b) * 64
                okv[k, b, a, 0] = dk[at:at + 64]
                okv[k, b, a, 1] = dv[at:at + 64]
        c_os(k).start()

    def stage_x(k):
        c_os(k).wait_recv()
        xb[k] = (okv[k, c, 1 - xh].astype(F32) + rsb[k, 1 - xh].astype(F32)).astype(BF16)
        c_ox(k).start()

    def loop_out(i, _):
        stage_out((i + 1) % 8)
        return 0

    lax.fori_loop(0, 8, loop_out, 0)

    def loop_x(i, _):
        stage_x((i + 1) % 8)
        return 0

    lax.fori_loop(0, 8, loop_x, 0)

    for d in range(1, 4):
        c_dy(d).wait_recv()

    def start_da(k, _):
        c_da(k).start()
        return 0

    lax.fori_loop(1, 8, start_da, 0)
    dx[s] = dr[s // 4, s % 4]

    def sums(k):
        for d in range(1, 4):
            c_oy(k, d).wait_recv()
        rb[k, 0:2] = (
            (oa[k, y].astype(F32) + ra[k, 1].astype(F32))
            + (ra[k, 2].astype(F32) + ra[k, 3].astype(F32))
        ).astype(BF16)
        c_ox(k).wait_recv()
        rb[k, 2:4] = (
            okv[k, c, xh].astype(F32) + rsb[k, xh].astype(F32) + rx[k].astype(F32)
        ).astype(BF16)

    def loop_sum(k, _):
        sums(k)
        c_ra(k).start()
        c_rk(k).start()
        return 0

    lax.fori_loop(1, 8, loop_sum, 0)
    sums(0)
    ret[s] = rb[0]

    def wait_ret(k, _):
        c_ra(k).wait_recv()
        c_rk(k).wait_recv()
        return 0

    lax.fori_loop(1, 8, wait_ret, 0)

    def unshuffle(t, q):
        return jnp.concatenate(
            [ret[h, t][:, q * 32:(q + 1) * 32] for h in range(8)], axis=-1
        )

    for q in range(8):
        rows = pl.ds(q * 64, 64)
        att = unshuffle(0, q).astype(F32)
        open_ = gate[rows, :]
        out = (open_ * att).astype(BF16)
        heads4[0, q] = out
        upd[q] = nn(out, ow[...]).astype(BF16)
        dpj[3, rows, :] = (gg[rows, :] * att * open_ * (1.0 - open_)).astype(BF16)
        for t in range(3):
            dpj[t, rows, :] = unshuffle(t + 1, q)
    for g in range(4):
        w = nn(nbt[...], dpj[g]).reshape(2, 8, 16, 256)
        ch[:, :, g * 16:(g + 1) * 16, :] = w
    w = tn(heads4[0].reshape(512, 256), ug[...].reshape(512, 256)).reshape(2, 8, 16, 256)
    ch[:, :, 64:80, :] = w

    def wait_da(k, _):
        c_da(k).wait_recv()
        return 0

    lax.fori_loop(1, 8, wait_da, 0)
    w_mean = jnp.mean(w_all, axis=-1, keepdims=True)
    v_hi, v_mid, _ = split3(w_all - w_mean)
    one_rows = jnp.where(
        lax.broadcasted_iota(jnp.int32, (8, 128), 0) < 2, 1.0, 0.0
    ).astype(BF16)
    zero_rows = jnp.zeros((8, 128), BF16)
    rhs = jnp.concatenate(
        [
            jnp.concatenate([v_hi, zero_rows], axis=1),
            jnp.concatenate([v_mid, zero_rows], axis=1),
            jnp.concatenate([v_hi, zero_rows], axis=1),
            jnp.concatenate([zero_rows, one_rows], axis=1),
        ],
        axis=0,
    )
    pwacc[...] = jnp.zeros_like(pwacc)

    def pair_back(k, _):
        base = pl.multiple_of(k * 1024, 1024)
        g = jnp.concatenate([dx[:, k * 8 + q, :] for q in range(8)], axis=1)
        b = jnp.concatenate([bs[:, k * 8 + q, :] for q in range(8)], axis=1)
        cross = jnp.sum(g * b, axis=0, keepdims=True) * (1.0 / 128)
        c_hi, c_lo = split2(cross)
        g_hi, g_lo = split2(g)
        tail = jnp.concatenate(
            [c_hi.astype(F32), c_lo.astype(F32), jnp.zeros((6, 1024), F32)], axis=0
        ).astype(BF16)
        lhs = jnp.concatenate([g_hi, g_hi, g_lo, tail], axis=0)
        both = tn(lhs, rhs)
        normed = xn[pl.ds(base, 1024), :]
        back = rst[pl.ds(base, 1024), :] * (both[:, 0:128] - normed * both[:, 128:256])
        pg[pl.ds(k * 8, 8)] = back.astype(BF16).reshape(8, 128, 128)
        n_hi, n_lo = split2(normed)
        g2 = jnp.concatenate([g_hi, g_lo], axis=0)
        part = nn(g2, n_hi) + nn(g2, n_lo)
        pwacc[...] += part[0:8] + part[8:16]
        return 0

    lax.fori_loop(0, 8, pair_back, 0)
    ch[:, :, 80:88, :] = jnp.zeros((2, 8, 8, 256), F32)
    ch[0, 0, 80:88, 0:128] = pwacc[...]

    c_tc().start()
    for q in range(8):
        rows = pl.ds(q * 64, 64)
        d = nt(dpj[0, rows, :], cw[:, 0:256])
        for g in range(1, 4):
            d += nt(dpj[g, rows, :], cw[:, g * 256:(g + 1) * 256])
        n = nf[rows, :]
        spread = spb[rows, 0:1]
        mean_d = jnp.mean(d, axis=-1, keepdims=True)
        mean_x = jnp.mean(d * n, axis=-1, keepdims=True)
        alg[q] = (spread * (d - mean_d - n * mean_x)).astype(BF16)
    c_tc().wait_recv()
    ch2[...] = ch[c] + chr_[...]

    def start_ts(k, _):
        c_ts(k).start()
        return 0

    lax.fori_loop(1, 8, start_ts, 0)
    acc = ch2[s]
    for k in range(1, 8):
        c_ts(k).wait_recv()
        acc += chs[k]
    chs[0] = acc
    c_tx().start()
    c_tx().wait_recv()
    acc += chx[0]
    chx[1] = acc
    for d in range(1, 4):
        c_ty(d).start()
    chy[0] = acc
    for d in range(1, 4):
        c_ty(d).wait_recv()
    acc = jnp.zeros((88, 256), F32)
    for a in range(4):
        acc += chy[(y + 4 - a) % 4]
    chf[c, s] = acc

    def start_as(k, _):
        c_as(k).start()
        return 0

    lax.fori_loop(1, 8, start_as, 0)
    for k in range(1, 8):
        c_as(k).wait_recv()
    c_ac().start()
    c_ac().wait_recv()
    for b in range(2):
        for q in range(8):
            at = (b * 8 + q) * 16
            for g in range(4):
                dcw[at:at + 16, g * 256:(g + 1) * 256] = chf[b, q, g * 16:(g + 1) * 16, :]
            dow[at:at + 16, :] = chf[b, q, 64:80, :]
    dpw[...] = chf[0, 0, 80:88, 0:128]

    def drain(k, _):
        c_in_qa(k).wait_send()
        c_in_kv(k).wait_send()
        c_pa(k).wait_send()
        c_ra(k).wait_send()
        c_rk(k).wait_send()
        c_da(k).wait_send()
        c_ts(k).wait_send()
        c_as(k).wait_send()
        return 0

    lax.fori_loop(1, 8, drain, 0)

    def drain_all(k, _):
        for d in range(1, 4):
            c_gy(k, d).wait_send()
            c_oy(k, d).wait_send()
        c_gx(k).wait_send()
        c_gs(k).wait_send()
        c_gf(k).wait_send()
        c_os(k).wait_send()
        c_ox(k).wait_send()
        return 0

    lax.fori_loop(0, 8, drain_all, 0)
    for d in range(1, 4):
        c_py(d).wait_send()
        c_st(d).wait_send()
        c_dy(d).wait_send()
        c_ty(d).wait_send()
    c_tc().wait_send()
    c_tx().wait_send()
    c_ac().wait_send()


def body(alignment_rows, pair_entries, combined_weight, output_weight, pair_weight, updated_gradient):
    V = pltpu.VMEM
    scratch = [
        V((512, 256), F32),
        V((512, 128), F32),
        V((512, 256), BF16),
        V((256, 512), BF16),
        V((512, 256), F32),
        V((512, 256), F32),
        V((4, 8, 64, 256), BF16),
        V((8, 4, 64, 256), BF16),
        V((8, 4, 2, 64, 256), BF16),
        V((8, 4, 2, 64, 256), BF16),
        V((8192, 128), F32),
        V((8192, 128), F32),
        V((8, 64, 128), F32),
        V((2, 4, 64, 128), F32),
        V((4, 2, 64, 128), F32),
        V((4, 256, 256), BF16),
        V((4, 8, 256), F32),
        V((256, 256), F32),
        V((256, 256), F32),
        V((8, 4, 2, 64, 256), BF16),
        V((8, 2, 2, 2, 64, 256), BF16),
        V((8, 4, 2, 64, 256), BF16),
        V((8, 2, 2, 64, 256), BF16),
        V((8, 2, 64, 256), BF16),
        V((8, 2, 64, 256), BF16),
        V((8, 4, 64, 256), BF16),
        V((8, 4, 64, 256), BF16),
        V((4, 2, 64, 128), F32),
        V((2, 4, 64, 128), F32),
        V((8, 64, 128), F32),
        V((4, 512, 256), BF16),
        V((2, 8, 88, 256), F32),
        V((8, 88, 256), F32),
        V((8, 88, 256), F32),
        V((8, 88, 256), F32),
        V((2, 88, 256), F32),
        V((4, 88, 256), F32),
        V((2, 8, 88, 256), F32),
        V((8, 128), F32),
        pltpu.SemaphoreType.DMA((SEM_COUNT,)),
        pltpu.SemaphoreType.DMA((SEM_COUNT,)),
    ]
    vm = pl.BlockSpec(memory_space=pltpu.VMEM)
    out = pl.pallas_call(
        kernel,
        out_shape=(
            jax.ShapeDtypeStruct((8, 64, 256), BF16),
            jax.ShapeDtypeStruct((8, 64, 256), BF16),
            jax.ShapeDtypeStruct((64, 128, 128), BF16),
            jax.ShapeDtypeStruct((256, 1024), F32),
            jax.ShapeDtypeStruct((256, 256), F32),
            jax.ShapeDtypeStruct((8, 128), F32),
        ),
        in_specs=[vm] * 6,
        out_specs=(vm,) * 6,
        scratch_shapes=scratch,
        compiler_params=pltpu.CompilerParams(
            collective_id=0, has_side_effects=True, vmem_limit_bytes=62 << 20
        ),
        name="row_attention",
    )(alignment_rows, pair_entries, combined_weight, output_weight, pair_weight.T, updated_gradient)
    return out[0], out[1], out[2], out[3], out[4], out[5].T


def solution(mesh):
    return jax.shard_map(
        body,
        mesh=mesh,
        in_specs=(
            P("seq", "res", None),
            P("res", "seq", None),
            P(),
            P(),
            P(),
            P("seq", "res", None),
        ),
        out_specs=(
            P("seq", "res", None),
            P("seq", "res", None),
            P("res", "seq", None),
            P(),
            P(),
            P(),
        ),
        check_vma=False,
    )
```

time: 692 us -> 143 us (0.21)
  waiting for transfers between devices: 450 us -> 0 us
  Pallas kernels: 0 us -> 133 us
  blocking collectives: 82.3 us -> 0 us
  local copies, waits for them, and re-layouts: 59.9 us -> 8.88 us
  matrix products: 49.5 us -> 0 us
  other arithmetic: 34.5 us -> 0 us
  between operations: 14 us -> 0.65 us
    psum x2 -> x0, waiting for transfers between devices: 328 us -> none  [the longest x1 181 us: body(): lax.psum(lax.dynamic_update_slice_in_dim(score_terms, own_block, col_star...]
    pallas_call x0 -> x1, Pallas kernels: none -> 133 us  [body(): pl.pallas_call(kernel, out_shape=(jax.ShapeDtypeStruct((8, 64, 256), BF16...]
    all_gather x2 -> x0, waiting for transfers between devices: 92.5 us -> none  [the longest x1 47.2 us: body(): lax.all_gather(key_rows, 'res', axis=1, tiled=True)]
    psum x1 -> x0, blocking collectives: 82.3 us -> none  [body(): lax.psum((qkvg_local, out_local, pair_w_local), ('seq', 'res'))]
    dot_general x15 -> x0, matrix products: 49.5 us -> none  [the longest x1 6.97 us: body(): jnp.einsum('hij,sihd->jshd', softmax_low, attended_grad_heads, preferred_...]
    reduce_scatter x1 -> x0, waiting for transfers between devices: 28 us -> none  [body(): lax.psum_scatter(jnp.concatenate([merge_heads(key_part), merge_heads(valu...]
    reshape x3 -> x0, local copies, waits for them, and re-layouts: 19.9 us -> none  [merge_heads(): tensor.reshape(tensor.shape[0], tensor.shape[1], tensor.shape[2] * tensor...]
    all_gather x2 -> x0, local copies, waits for them, and re-layouts: 12.9 us -> none  [the longest x1 6.45 us: body(): lax.all_gather(key_rows, 'res', axis=1, tiled=True)]
  transfers between devices with their start and end apart: 5 -> 0, of which waited for: 5 -> 0; matrix products, arithmetic and copies ran while one was open for 9% -> 0% of each run, Pallas kernels for 0% -> 0%
where the time goes in v1:
time: 143 us
  Pallas kernels  133 us (93%)
  local copies, waits for them, and re-layouts  8.88 us (6%)
    pallas_call x1, Pallas kernels, body(): pl.pallas_call(kernel, out_shape=(jax.ShapeDtypeStruct((8, 64, 256), BF16...  133 us
    unnamed x12, local copies, waits for them, and re-layouts  8.88 us

profile of v1, /device:TPU:1, one launch (start us, length us, event | category | flops | bytes accessed | tf_op | source)
XLA Modules:
  0.0 142.8 jit_solution(12038034005273584204)
XLA Ops:
  0.6 133.2 %row_attention.1 = (bf16[8,64,256]{2,1,0:T(8,128)(2,1)}, bf16[8,64,256]{2,1,0:T(8,128)(2,1)}, bf16[64,128,128]{2,1,0:T(8,128)(2,1)}, f32[256,1024]{1,0:T(8,128)}, f32[256,256]{1,0:T(8,128)}, /*index=5*/f32[8,128]{1,0:T(8,128)}) custom-call(bf16[8,64,256]{2,1,0:T(8,128)(2,1)} %al.1, bf16[64,128,128]{2,1,0:T(8,128)(2,1)} %pe.1, bf16[256,1024]{1,0:T(8,128)(2,1)} %cw.1, ...), custom_call_target="tpu_custom_call" | custom-call | tf_op jit(solution)/shard_map/row_attention/pallas_call | solution.py:594
  133.9 1.7 %copy.18 = bf16[8,64,256]{2,1,0:T(8,128)(2,1)} copy(bf16[8,64,256]{2,1,0:T(8,128)(2,1)} %get-tuple-element.24) | data formatting | bytes 524288
  135.5 1.7 %copy.19 = bf16[8,64,256]{2,1,0:T(8,128)(2,1)} copy(bf16[8,64,256]{2,1,0:T(8,128)(2,1)} %get-tuple-element.25) | data formatting | bytes 524288
  137.2 0.0 copy-start
  137.2 0.0 copy-start.1
  137.2 3.3 %copy.20 = bf16[64,128,128]{2,1,0:T(8,128)(2,1)} copy(bf16[64,128,128]{2,1,0:T(8,128)(2,1)} %get-tuple-element.26) | data formatting | bytes 4194304
  140.5 0.0 copy-done
  140.5 0.0 copy-start.2
  140.5 1.0 copy.21
  141.4 0.0 copy-done.1
  141.5 0.7 copy.22
  142.2 0.0 copy-done.2
  142.2 0.6 copy.23
Async XLA Ops:
  137.2 3.3 %copy-start = (f32[256,1024]{1,0:T(8,128)S(1)}, f32[256,1024]{1,0:T(8,128)}, u32[]{:S(2)}) copy-start(f32[256,1024]{1,0:T(8,128)} %get-tuple-element.27) | copy-start | bytes 3145732
  137.2 4.2 %copy-start.1 = (f32[256,256]{1,0:T(8,128)S(1)}, f32[256,256]{1,0:T(8,128)}, u32[]{:S(2)}) copy-start(f32[256,256]{1,0:T(8,128)} %get-tuple-element.28) | copy-start | bytes 786436
  140.5 1.7 %copy-start.2 = (f32[8,128]{1,0:T(8,128)S(1)}, f32[8,128]{1,0:T(8,128)}, u32[]{:S(2)}) copy-start(f32[8,128]{1,0:T(8,128)} %get-tuple-element.17) | copy-start | bytes 12292

commit v2 on v1

--- a/solution.py
+++ b/solution.py
@@ -17,8 +17,8 @@
 PB_A, PB_Y, STAT = 72, 80, 84
 OY, OS, OX, RT_A, RT_K = 88, 120, 128, 136, 144
 DL_Y, DL_A = 152, 156
-T_C, T_S, T_X, T_Y, T_AS, T_AC = 164, 165, 173, 174, 178, 186
-SEM_COUNT = 187
+T_C, T_S, T_XY, T_AS, T_AC = 164, 165, 173, 181, 189
+SEM_COUNT = 190
 
 
 def nt(a, b):
@@ -48,12 +48,12 @@
 
 
 def kernel(
-    al, pe, cw, ow, pwt, ug,
-    upd, alg, pg, dcw, dow, dpw,
+    al, pe_in, cw, ow, pw, ug,
+    upd, alg, pg_out, chf,
     nf, spb, nb, nbt, gate, gg, heads4, sb, qa, kv,
     xn, rst, bs, pb, bi, bt, st, lt, dpt, oa, okv, ra, rsb, xb, rx, rb, ret,
-    dl, dr, dx, dpj, ch, chr_, ch2, chs, chx, chy, chf, pwacc,
-    ssem, rsem,
+    dl, dr, dx, dpj, ch, chr_, ch2, chs, chx, chy, pwacc,
+    pe, pg, ssem, rsem, lsem,
 ):
     s = lax.axis_index("seq")
     r = lax.axis_index("res")
@@ -70,6 +70,9 @@
     def at_y(d):
         return {"res": xh * 8 + ((y + d) % 4) * 2 + c}
 
+    def at_xy(m):
+        return {"res": ((xh + m // 4) % 2) * 8 + ((y + m) % 4) * 2 + c}
+
     at_x = {"res": (1 - xh) * 8 + y * 2 + c}
     at_c = {"res": xh * 8 + y * 2 + (1 - c)}
 
@@ -79,12 +82,13 @@
             device_id=where, device_id_type=MESH,
         )
 
+    load = pltpu.make_async_copy(pe_in, pe, lsem.at[8])
+    load.start()
+
     bar = pltpu.get_barrier_semaphore()
     for k in range(1, 8):
         pl.semaphore_signal(bar, inc=1, device_id=at_seq(k), device_id_type=MESH)
-    for d in range(1, 4):
-        pl.semaphore_signal(bar, inc=1, device_id=at_y(d), device_id_type=MESH)
-    pl.semaphore_signal(bar, inc=1, device_id=at_x, device_id_type=MESH)
+        pl.semaphore_signal(bar, inc=1, device_id=at_xy(k), device_id_type=MESH)
     pl.semaphore_signal(bar, inc=1, device_id=at_c, device_id_type=MESH)
 
     def c_in_qa(k):
@@ -144,11 +148,8 @@
     def c_ts(k):
         return send(ch2.at[at_seq(k)["seq"]], chs.at[k], T_S + k, at_seq(k))
 
-    def c_tx():
-        return send(chs.at[0], chx.at[0], T_X, at_x)
-
-    def c_ty(d):
-        return send(chx.at[1], chy.at[d], T_Y + d, at_y(d))
+    def c_txy(m):
+        return send(chx, chy.at[xh * 4 + y], T_XY + m, at_xy(m))
 
     def c_as(k):
         return send(chf.at[c, s], chf.at[c, s], T_AS + k, at_seq(k))
@@ -165,6 +166,12 @@
         nf[rows, :] = normed
         spb[rows, :] = jnp.broadcast_to(spread, (64, 128))
         nb[rows, :] = normed.astype(BF16)
+    def shuffle(t):
+        for h in range(8):
+            sb[h, t] = jnp.concatenate(
+                [heads4[t, q][:, h * 32:(h + 1) * 32] for q in range(8)], axis=-1
+            )
+
     for q in range(8):
         rows = pl.ds(q * 64, 64)
         n = nb[rows, :]
@@ -181,8 +188,7 @@
             sb[h, t] = jnp.concatenate(
                 [heads4[t, q][:, h * 32:(h + 1) * 32] for q in range(8)], axis=-1
             )
-
-    pl.semaphore_wait(bar, 12)
+    pl.semaphore_wait(bar, 15)
 
     def start_in(k, _):
         c_in_qa(k).start()
@@ -192,15 +198,14 @@
     lax.fori_loop(1, 8, start_in, 0)
     qa[0, y] = sb[s, 0:2]
     kv[0, p] = sb[s, 2:4]
-
-    def forward(k):
-        for d in (1, 3, 2):
-            c_gy(k, d).start()
-        c_gx(k).start()
-        c_gs(k).start()
-
+    c_gx(0).start()
+    c_gs(0).start()
+    for d in (1, 3, 2):
+        c_gy(0, d).start()
+
+    load.wait()
     ones = jnp.ones((128, 128), BF16)
-    w_all = pwt[...]
+    w_all = pw[...]
     w3 = jnp.concatenate(split3(w_all), axis=0)
 
     def pair_chunk(k):
@@ -218,21 +223,18 @@
         for q in range(8):
             bs[:, k * 8 + q, :] = b[:, q * 128:(q + 1) * 128]
 
-    forward(0)
-    pair_chunk(0)
-
     def stage_in(k, _):
         c_in_qa(k).wait_recv()
+        for d in (1, 3, 2):
+            c_gy(k, d).start()
         c_in_kv(k).wait_recv()
-        forward(k)
-        c_gx(k - 1).wait_recv()
-        c_gf(k - 1).start()
+        c_gx(k).start()
+        c_gs(k).start()
         pair_chunk(k)
         return 0
 
     lax.fori_loop(1, 8, stage_in, 0)
-    c_gx(7).wait_recv()
-    c_gf(7).start()
+    pair_chunk(0)
 
     def start_pair(k, _):
         c_pa(k).start()
@@ -240,6 +242,13 @@
 
     lax.fori_loop(1, 8, start_pair, 0)
     pb[s // 4, s % 4] = bs[s]
+
+    def share_x(k, _):
+        c_gx(k).wait_recv()
+        c_gf(k).start()
+        return 0
+
+    lax.fori_loop(0, 8, share_x, 0)
     nbt[...] = nb[...].T
 
     def wait_pair(k, _):
@@ -251,8 +260,13 @@
         c_py(d).start()
     bi[y] = pb[:, y]
 
-    lt[...] = jnp.zeros_like(lt)
     dpt[...] = jnp.zeros_like(dpt)
+    for d in range(1, 4):
+        c_py(d).wait_recv()
+    bias = jnp.concatenate(
+        [jnp.concatenate([bi[a, b] for a in range(4)], axis=0) for b in range(2)], axis=1
+    )
+    lt[...] = bias.T
 
     def stage_mm(k, _):
         for d in range(1, 4):
@@ -268,12 +282,7 @@
         return 0
 
     lax.fori_loop(0, 8, stage_mm, 0)
-    for d in range(1, 4):
-        c_py(d).wait_recv()
-    bias = jnp.concatenate(
-        [jnp.concatenate([bi[a, b] for a in range(4)], axis=0) for b in range(2)], axis=1
-    )
-    logits = lt[...] + bias.T
+    logits = lt[...]
     top = jnp.max(logits, axis=0, keepdims=True)
     e = jnp.exp(logits - top)
     dp = dpt[...]
@@ -336,17 +345,15 @@
         xb[k] = (okv[k, c, 1 - xh].astype(F32) + rsb[k, 1 - xh].astype(F32)).astype(BF16)
         c_ox(k).start()
 
+    stage_out(1)
+
     def loop_out(i, _):
         stage_out((i + 1) % 8)
-        return 0
-
-    lax.fori_loop(0, 8, loop_out, 0)
-
-    def loop_x(i, _):
-        stage_x((i + 1) % 8)
-        return 0
-
-    lax.fori_loop(0, 8, loop_x, 0)
+        stage_x(i)
+        return 0
+
+    lax.fori_loop(1, 8, loop_out, 0)
+    stage_x(0)
 
     for d in range(1, 4):
         c_dy(d).wait_recv()
@@ -357,56 +364,6 @@
 
     lax.fori_loop(1, 8, start_da, 0)
     dx[s] = dr[s // 4, s % 4]
-
-    def sums(k):
-        for d in range(1, 4):
-            c_oy(k, d).wait_recv()
-        rb[k, 0:2] = (
-            (oa[k, y].astype(F32) + ra[k, 1].astype(F32))
-            + (ra[k, 2].astype(F32) + ra[k, 3].astype(F32))
-        ).astype(BF16)
-        c_ox(k).wait_recv()
-        rb[k, 2:4] = (
-            okv[k, c, xh].astype(F32) + rsb[k, xh].astype(F32) + rx[k].astype(F32)
-        ).astype(BF16)
-
-    def loop_sum(k, _):
-        sums(k)
-        c_ra(k).start()
-        c_rk(k).start()
-        return 0
-
-    lax.fori_loop(1, 8, loop_sum, 0)
-    sums(0)
-    ret[s] = rb[0]
-
-    def wait_ret(k, _):
-        c_ra(k).wait_recv()
-        c_rk(k).wait_recv()
-        return 0
-
-    lax.fori_loop(1, 8, wait_ret, 0)
-
-    def unshuffle(t, q):
-        return jnp.concatenate(
-            [ret[h, t][:, q * 32:(q + 1) * 32] for h in range(8)], axis=-1
-        )
-
-    for q in range(8):
-        rows = pl.ds(q * 64, 64)
-        att = unshuffle(0, q).astype(F32)
-        open_ = gate[rows, :]
-        out = (open_ * att).astype(BF16)
-        heads4[0, q] = out
-        upd[q] = nn(out, ow[...]).astype(BF16)
-        dpj[3, rows, :] = (gg[rows, :] * att * open_ * (1.0 - open_)).astype(BF16)
-        for t in range(3):
-            dpj[t, rows, :] = unshuffle(t + 1, q)
-    for g in range(4):
-        w = nn(nbt[...], dpj[g]).reshape(2, 8, 16, 256)
-        ch[:, :, g * 16:(g + 1) * 16, :] = w
-    w = tn(heads4[0].reshape(512, 256), ug[...].reshape(512, 256)).reshape(2, 8, 16, 256)
-    ch[:, :, 64:80, :] = w
 
     def wait_da(k, _):
         c_da(k).wait_recv()
@@ -430,7 +387,11 @@
     )
     pwacc[...] = jnp.zeros_like(pwacc)
 
-    def pair_back(k, _):
+    def store(k):
+        rows = pl.ds(k * 8, 8)
+        return pltpu.make_async_copy(pg.at[rows], pg_out.at[rows], lsem.at[k])
+
+    def pair_back(k):
         base = pl.multiple_of(k * 1024, 1024)
         g = jnp.concatenate([dx[:, k * 8 + q, :] for q in range(8)], axis=1)
         b = jnp.concatenate([bs[:, k * 8 + q, :] for q in range(8)], axis=1)
@@ -445,17 +406,76 @@
         normed = xn[pl.ds(base, 1024), :]
         back = rst[pl.ds(base, 1024), :] * (both[:, 0:128] - normed * both[:, 128:256])
         pg[pl.ds(k * 8, 8)] = back.astype(BF16).reshape(8, 128, 128)
+        store(k).start()
         n_hi, n_lo = split2(normed)
         g2 = jnp.concatenate([g_hi, g_lo], axis=0)
         part = nn(g2, n_hi) + nn(g2, n_lo)
         pwacc[...] += part[0:8] + part[8:16]
-        return 0
-
-    lax.fori_loop(0, 8, pair_back, 0)
-    ch[:, :, 80:88, :] = jnp.zeros((2, 8, 8, 256), F32)
+
+    def sums(k):
+        for d in range(1, 4):
+            c_oy(k, d).wait_recv()
+        rb[k, 0:2] = (
+            (oa[k, y].astype(F32) + ra[k, 1].astype(F32))
+            + (ra[k, 2].astype(F32) + ra[k, 3].astype(F32))
+        ).astype(BF16)
+        c_ox(k).wait_recv()
+        rb[k, 2:4] = (
+            okv[k, c, xh].astype(F32) + rsb[k, xh].astype(F32) + rx[k].astype(F32)
+        ).astype(BF16)
+
+    def loop_sum(k, _):
+        sums(k)
+        c_ra(k).start()
+        c_rk(k).start()
+        pair_back(k)
+        return 0
+
+    lax.fori_loop(1, 8, loop_sum, 0)
+    sums(0)
+    ret[s] = rb[0]
+    pair_back(0)
+
+    def wait_ret(k, _):
+        c_ra(k).wait_recv()
+        c_rk(k).wait_recv()
+        return 0
+
+    lax.fori_loop(1, 8, wait_ret, 0)
+
+    def unshuffle(t, q):
+        return jnp.concatenate(
+            [ret[h, t][:, q * 32:(q + 1) * 32] for h in range(8)], axis=-1
+        )
+
+    for q in range(8):
+        rows = pl.ds(q * 64, 64)
+        att = unshuffle(0, q).astype(F32)
+        open_ = gate[rows, :]
+        out = (open_ * att).astype(BF16)
+        heads4[0, q] = out
+        upd[q] = nn(out, ow[...]).astype(BF16)
+        dpj[3, rows, :] = (gg[rows, :] * att * open_ * (1.0 - open_)).astype(BF16)
+        for t in range(3):
+            dpj[t, rows, :] = unshuffle(t + 1, q)
+    for g in range(4):
+        w = nn(nbt[...], dpj[g]).reshape(2, 8, 16, 256)
+        ch[:, :, g * 16:(g + 1) * 16, :] = w
+    w = tn(heads4[0].reshape(512, 256), ug[...].reshape(512, 256)).reshape(2, 8, 16, 256)
+    ch[:, :, 64:80, :] = w
+
+    ch[:, :, 80:96, :] = jnp.zeros((2, 8, 16, 256), F32)
     ch[0, 0, 80:88, 0:128] = pwacc[...]
 
     c_tc().start()
+    c_tc().wait_recv()
+    ch2[...] = (ch[c] + chr_[...]).astype(BF16)
+
+    def start_ts(k, _):
+        c_ts(k).start()
+        return 0
+
+    lax.fori_loop(1, 8, start_ts, 0)
     for q in range(8):
         rows = pl.ds(q * 64, 64)
         d = nt(dpj[0, rows, :], cw[:, 0:256])
@@ -466,32 +486,24 @@
         mean_d = jnp.mean(d, axis=-1, keepdims=True)
         mean_x = jnp.mean(d * n, axis=-1, keepdims=True)
         alg[q] = (spread * (d - mean_d - n * mean_x)).astype(BF16)
-    c_tc().wait_recv()
-    ch2[...] = ch[c] + chr_[...]
-
-    def start_ts(k, _):
-        c_ts(k).start()
-        return 0
-
-    lax.fori_loop(1, 8, start_ts, 0)
-    acc = ch2[s]
+    acc = ch2[s].astype(F32)
     for k in range(1, 8):
         c_ts(k).wait_recv()
-        acc += chs[k]
-    chs[0] = acc
-    c_tx().start()
-    c_tx().wait_recv()
-    acc += chx[0]
-    chx[1] = acc
-    for d in range(1, 4):
-        c_ty(d).start()
-    chy[0] = acc
-    for d in range(1, 4):
-        c_ty(d).wait_recv()
-    acc = jnp.zeros((88, 256), F32)
-    for a in range(4):
-        acc += chy[(y + 4 - a) % 4]
-    chf[c, s] = acc
+        acc += chs[k].astype(F32)
+    chx[...] = acc.astype(BF16)
+    chy[xh * 4 + y] = chx[...]
+
+    def start_xy(m, _):
+        c_txy(m).start()
+        return 0
+
+    lax.fori_loop(1, 8, start_xy, 0)
+    for m in range(1, 8):
+        c_txy(m).wait_recv()
+    acc = chy[0].astype(F32)
+    for a in range(1, 8):
+        acc += chy[a].astype(F32)
+    chf[c, s] = acc.astype(BF16)
 
     def start_as(k, _):
         c_as(k).start()
@@ -502,13 +514,6 @@
         c_as(k).wait_recv()
     c_ac().start()
     c_ac().wait_recv()
-    for b in range(2):
-        for q in range(8):
-            at = (b * 8 + q) * 16
-            for g in range(4):
-                dcw[at:at + 16, g * 256:(g + 1) * 256] = chf[b, q, g * 16:(g + 1) * 16, :]
-            dow[at:at + 16, :] = chf[b, q, 64:80, :]
-    dpw[...] = chf[0, 0, 80:88, 0:128]
 
     def drain(k, _):
         c_in_qa(k).wait_send()
@@ -519,9 +524,12 @@
         c_da(k).wait_send()
         c_ts(k).wait_send()
         c_as(k).wait_send()
+        c_txy(k).wait_send()
         return 0
 
     lax.fori_loop(1, 8, drain, 0)
+    for k in range(8):
+        store(k).wait()
 
     def drain_all(k, _):
         for d in range(1, 4):
@@ -539,10 +547,30 @@
         c_py(d).wait_send()
         c_st(d).wait_send()
         c_dy(d).wait_send()
-        c_ty(d).wait_send()
     c_tc().wait_send()
-    c_tx().wait_send()
     c_ac().wait_send()
+
+
+def finish(upd_in, alg_in, pg_in, chf, upd, alg, pg, dcw, dow, dpw, tok, pair, isem, osem):
+    moves = [(pg_in.at[pl.ds(16 * a, 16)], pair.at[a], pg.at[pl.ds(16 * a, 16)]) for a in range(4)]
+    moves.append((upd_in, tok.at[0], upd))
+    moves.append((alg_in, tok.at[1], alg))
+    reads = [pltpu.make_async_copy(m[0], m[1], isem.at[i]) for i, m in enumerate(moves)]
+    writes = [pltpu.make_async_copy(m[1], m[2], osem.at[i]) for i, m in enumerate(moves)]
+    for copy in reads:
+        copy.start()
+    for b in range(2):
+        for q in range(8):
+            at = (b * 8 + q) * 16
+            for g in range(4):
+                dcw[at:at + 16, g * 256:(g + 1) * 256] = chf[b, q, g * 16:(g + 1) * 16, :].astype(F32)
+            dow[at:at + 16, :] = chf[b, q, 64:80, :].astype(F32)
+    dpw[...] = chf[0, 0, 80:96, 0:128].astype(F32)[0:8]
+    for read, write in zip(reads, writes):
+        read.wait()
+        write.start()
+    for copy in writes:
+        copy.wait()
 
 
 def body(alignment_rows, pair_entries, combined_weight, output_weight, pair_weight, updated_gradient):
@@ -579,37 +607,56 @@
         V((2, 4, 64, 128), F32),
         V((8, 64, 128), F32),
         V((4, 512, 256), BF16),
-        V((2, 8, 88, 256), F32),
-        V((8, 88, 256), F32),
-        V((8, 88, 256), F32),
-        V((8, 88, 256), F32),
-        V((2, 88, 256), F32),
-        V((4, 88, 256), F32),
-        V((2, 8, 88, 256), F32),
+        V((2, 8, 96, 256), F32),
+        V((8, 96, 256), F32),
+        V((8, 96, 256), BF16),
+        V((8, 96, 256), BF16),
+        V((96, 256), BF16),
+        V((8, 96, 256), BF16),
         V((8, 128), F32),
+        V((64, 128, 128), BF16),
+        V((64, 128, 128), BF16),
         pltpu.SemaphoreType.DMA((SEM_COUNT,)),
         pltpu.SemaphoreType.DMA((SEM_COUNT,)),
+        pltpu.SemaphoreType.DMA((9,)),
     ]
     vm = pl.BlockSpec(memory_space=pltpu.VMEM)
-    out = pl.pallas_call(
+    hbm = pl.BlockSpec(memory_space=pl.ANY)
+    tokens = jax.ShapeDtypeStruct((8, 64, 256), BF16)
+    pairs = jax.ShapeDtypeStruct((64, 128, 128), BF16)
+    upd, alg, pg, chf = pl.pallas_call(
         kernel,
+        out_shape=(tokens, tokens, pairs, jax.ShapeDtypeStruct((2, 8, 96, 256), BF16)),
+        in_specs=[vm, hbm, vm, vm, vm, vm],
+        out_specs=(vm, vm, hbm, vm),
+        scratch_shapes=scratch,
+        compiler_params=pltpu.CompilerParams(
+            collective_id=0, has_side_effects=True, vmem_limit_bytes=60 << 20
+        ),
+        name="row_attention",
+    )(alignment_rows, pair_entries, combined_weight, output_weight, pair_weight.T, updated_gradient)
+    done = pl.pallas_call(
+        finish,
         out_shape=(
-            jax.ShapeDtypeStruct((8, 64, 256), BF16),
-            jax.ShapeDtypeStruct((8, 64, 256), BF16),
-            jax.ShapeDtypeStruct((64, 128, 128), BF16),
+            tokens,
+            tokens,
+            pairs,
             jax.ShapeDtypeStruct((256, 1024), F32),
             jax.ShapeDtypeStruct((256, 256), F32),
             jax.ShapeDtypeStruct((8, 128), F32),
         ),
-        in_specs=[vm] * 6,
-        out_specs=(vm,) * 6,
-        scratch_shapes=scratch,
-        compiler_params=pltpu.CompilerParams(
-            collective_id=0, has_side_effects=True, vmem_limit_bytes=62 << 20
-        ),
-        name="row_attention",
-    )(alignment_rows, pair_entries, combined_weight, output_weight, pair_weight.T, updated_gradient)
-    return out[0], out[1], out[2], out[3], out[4], out[5].T
+        in_specs=[hbm, hbm, hbm, vm],
+        out_specs=(hbm, hbm, hbm, vm, vm, vm),
+        scratch_shapes=[
+            V((2, 8, 64, 256), BF16),
+            V((4, 16, 128, 128), BF16),
+            pltpu.SemaphoreType.DMA((6,)),
+            pltpu.SemaphoreType.DMA((6,)),
+        ],
+        compiler_params=pltpu.CompilerParams(vmem_limit_bytes=60 << 20),
+        name="results",
+    )(upd, alg, pg, chf)
+    return *done[:5], done[5].T
 
 
 def solution(mesh):

time: 143 us -> 118 us (0.83)
  Pallas kernels: 133 us -> 117 us
  local copies, waits for them, and re-layouts: 8.88 us -> 0 us
    pallas_call x1 -> x2, Pallas kernels: 133 us -> 117 us  [the longest x1 113 us: body(): pl.pallas_call(kernel, out_shape=(tokens, tokens, pairs, jax.ShapeDtypeSt...]
    unnamed x12 -> x0, local copies, waits for them, and re-layouts: 8.88 us -> none
where the time goes in v2:
time: 118 us
  Pallas kernels  117 us (99%)
    pallas_call x1, Pallas kernels, body(): pl.pallas_call(kernel, out_shape=(tokens, tokens, pairs, jax.ShapeDtypeSt...  113 us
    pallas_call x1, Pallas kernels, body(): pl.pallas_call(finish, out_shape=(tokens, tokens, pairs, jax.ShapeDtypeSt...  4.82 us

profile of v2, /device:TPU:1, one launch (start us, length us, event | category | flops | bytes accessed | tf_op | source)
XLA Modules:
  0.0 118.1 jit_solution(18293356679923286561)
XLA Ops:
  0.6 112.6 %row_attention.1 = (bf16[8,64,256]{2,1,0:T(8,128)(2,1)}, bf16[8,64,256]{2,1,0:T(8,128)(2,1)}, bf16[64,128,128]{2,1,0:T(8,128)(2,1)}, bf16[2,8,96,256]{3,2,1,0:T(8,128)(2,1)}) custom-call(bf16[8,64,256]{2,1,0:T(8,128)(2,1)} %al.1, bf16[64,128,128]{2,1,0:T(8,128)(2,1)} %pe_in.1, bf16[256,1024]{1,0:T(8,128)(2,1)} %cw.1, bf16[256,256]{1,0:T(8,128)(2,1)} %ow.1, ...), custom_call_target="tpu_custom_call" | custom-call | tf_op jit(solution)/shard_map/row_attention/pallas_call | solution.py:627
  113.3 4.8 %results.1 = (bf16[8,64,256]{2,1,0:T(8,128)(2,1)}, bf16[8,64,256]{2,1,0:T(8,128)(2,1)}, bf16[64,128,128]{2,1,0:T(8,128)(2,1)}, f32[256,1024]{1,0:T(8,128)}, f32[256,256]{1,0:T(8,128)}, /*index=5*/f32[8,128]{1,0:T(8,128)}) custom-call(bf16[8,64,256]{2,1,0:T(8,128)(2,1)} %get-tuple-element.16.upd_in, bf16[8,64,256]{2,1,0:T(8,128)(2,1)} %get-tuple-element.17.alg_in, ...), custom_call_target="tpu_custom_call" | custom-call | tf_op jit(solution)/shard_map/results/pallas_call | solution.py:638

commit v3 on v2

--- a/solution.py
+++ b/solution.py
@@ -19,6 +19,7 @@
 DL_Y, DL_A = 152, 156
 T_C, T_S, T_XY, T_AS, T_AC = 164, 165, 173, 181, 189
 SEM_COUNT = 190
+LAG = 2
 
 
 def nt(a, b):
@@ -48,12 +49,12 @@
 
 
 def kernel(
-    al, pe_in, cw, ow, pw, ug,
-    upd, alg, pg_out, chf,
+    al_in, pe_in, cw_in, ow_in, pw_in, ug_in,
+    upd_out, alg_out, pg_out, chf_out,
     nf, spb, nb, nbt, gate, gg, heads4, sb, qa, kv,
     xn, rst, bs, pb, bi, bt, st, lt, dpt, oa, okv, ra, rsb, xb, rx, rb, ret,
     dl, dr, dx, dpj, ch, chr_, ch2, chs, chx, chy, pwacc,
-    pe, pg, ssem, rsem, lsem,
+    al, pe, cw, ow, pw, ug, upd, alg, pg, chf, ssem, rsem, lsem,
 ):
     s = lax.axis_index("seq")
     r = lax.axis_index("res")
@@ -82,8 +83,14 @@
             device_id=where, device_id_type=MESH,
         )
 
-    load = pltpu.make_async_copy(pe_in, pe, lsem.at[8])
-    load.start()
+    loads = [
+        pltpu.make_async_copy(a, b, lsem.at[8 + i])
+        for i, (a, b) in enumerate(
+            ((al_in, al), (cw_in, cw), (ug_in, ug), (ow_in, ow), (pw_in, pw), (pe_in, pe))
+        )
+    ]
+    for load in loads:
+        load.start()
 
     bar = pltpu.get_barrier_semaphore()
     for k in range(1, 8):
@@ -100,6 +107,11 @@
     def c_gy(k, d):
         return send(qa.at[k, y], qa.at[k, y], GY + k * 4 + d, at_y(d))
 
+    def c_gr(k, d):
+        t = 0 if d == 1 else 1
+        src = qa.at[k, (y + 4 - d) % 4, t]
+        return send(src, src, GY + k * 4 + (0 if d == 1 else 2), at_y(d))
+
     def c_gx(k):
         return send(kv.at[k, p], kv.at[k, p], GX + k, at_x)
 
@@ -119,6 +131,13 @@
 
     def c_st(d):
         return send(st.at[y], st.at[y], STAT + d, at_y(d))
+
+    def c_or(k, d):
+        t = 0 if d == 1 else 1
+        return send(
+            oa.at[k, (y + 2) % 4, t], ra.at[k, 0 if d == 1 else 2, 0],
+            OY + k * 4 + (0 if d == 1 else 2), at_y(d),
+        )
 
     def c_oy(k, d):
         return send(oa.at[k, (y + d) % 4], ra.at[k, d], OY + k * 4 + d, at_y(d))
@@ -157,6 +176,7 @@
     def c_ac():
         return send(chf.at[c], chf.at[c], T_AC, at_c)
 
+    loads[0].wait()
     for q in range(8):
         x = al[q].astype(F32)
         cen = x - jnp.mean(x, axis=-1, keepdims=True)
@@ -172,6 +192,8 @@
                 [heads4[t, q][:, h * 32:(h + 1) * 32] for q in range(8)], axis=-1
             )
 
+    for load in loads[1:4]:
+        load.wait()
     for q in range(8):
         rows = pl.ds(q * 64, 64)
         n = nb[rows, :]
@@ -200,10 +222,11 @@
     kv[0, p] = sb[s, 2:4]
     c_gx(0).start()
     c_gs(0).start()
-    for d in (1, 3, 2):
+    for d in (1, 3):
         c_gy(0, d).start()
 
-    load.wait()
+    for load in loads[4:]:
+        load.wait()
     ones = jnp.ones((128, 128), BF16)
     w_all = pw[...]
     w3 = jnp.concatenate(split3(w_all), axis=0)
@@ -225,7 +248,7 @@
 
     def stage_in(k, _):
         c_in_qa(k).wait_recv()
-        for d in (1, 3, 2):
+        for d in (1, 3):
             c_gy(k, d).start()
         c_in_kv(k).wait_recv()
         c_gx(k).start()
@@ -244,6 +267,9 @@
     pb[s // 4, s % 4] = bs[s]
 
     def share_x(k, _):
+        for d in (1, 3):
+            c_gy(k, d).wait_recv()
+            c_gr(k, d).start()
         c_gx(k).wait_recv()
         c_gf(k).start()
         return 0
@@ -269,8 +295,8 @@
     lt[...] = bias.T
 
     def stage_mm(k, _):
-        for d in range(1, 4):
-            c_gy(k, d).wait_recv()
+        for d in (1, 3):
+            c_gr(k, d).wait_recv()
         c_gs(k).wait_recv()
         c_gf(k).wait_recv()
         qk = qa[k, :, 0].reshape(256, 256)
@@ -329,8 +355,8 @@
         vk = kv[k, :, 1].reshape(256, 256)
         oa[k, :, 0] = nn(bt[1], vk).astype(BF16).reshape(4, 64, 256)
         oa[k, :, 1] = (nn(bt[3], kk) * SCALE).astype(BF16).reshape(4, 64, 256)
-        for d in (1, 3, 2):
-            c_oy(k, d).start()
+        for d in (1, 3):
+            c_or(k, d).start()
         dk = nn(bt[2], qk).astype(BF16)
         dv = nn(bt[0], dak).astype(BF16)
         for a in range(2):
@@ -340,6 +366,16 @@
                 okv[k, b, a, 1] = dv[at:at + 64]
         c_os(k).start()
 
+    def stage_y(k):
+        for d in (1, 3):
+            t = 0 if d == 1 else 1
+            c_or(k, d).wait_recv()
+            to = (y + d) % 4
+            oa[k, to, t] = (
+                oa[k, to, t].astype(F32) + ra[k, 0 if d == 1 else 2, 0].astype(F32)
+            ).astype(BF16)
+            c_oy(k, d).start()
+
     def stage_x(k):
         c_os(k).wait_recv()
         xb[k] = (okv[k, c, 1 - xh].astype(F32) + rsb[k, 1 - xh].astype(F32)).astype(BF16)
@@ -350,10 +386,17 @@
     def loop_out(i, _):
         stage_out((i + 1) % 8)
         stage_x(i)
+
+        @pl.when(i > LAG)
+        def _relay():
+            stage_y(i - LAG)
+
         return 0
 
     lax.fori_loop(1, 8, loop_out, 0)
     stage_x(0)
+    for i in range(8 - LAG, 9):
+        stage_y(i % 8)
 
     for d in range(1, 4):
         c_dy(d).wait_recv()
@@ -391,7 +434,7 @@
         rows = pl.ds(k * 8, 8)
         return pltpu.make_async_copy(pg.at[rows], pg_out.at[rows], lsem.at[k])
 
-    def pair_back(k):
+    def pair_back(k, _):
         base = pl.multiple_of(k * 1024, 1024)
         g = jnp.concatenate([dx[:, k * 8 + q, :] for q in range(8)], axis=1)
         b = jnp.concatenate([bs[:, k * 8 + q, :] for q in range(8)], axis=1)
@@ -411,13 +454,13 @@
         g2 = jnp.concatenate([g_hi, g_lo], axis=0)
         part = nn(g2, n_hi) + nn(g2, n_lo)
         pwacc[...] += part[0:8] + part[8:16]
+        return 0
 
     def sums(k):
-        for d in range(1, 4):
+        for d in (1, 3):
             c_oy(k, d).wait_recv()
         rb[k, 0:2] = (
-            (oa[k, y].astype(F32) + ra[k, 1].astype(F32))
-            + (ra[k, 2].astype(F32) + ra[k, 3].astype(F32))
+            oa[k, y].astype(F32) + (ra[k, 1].astype(F32) + ra[k, 3].astype(F32))
         ).astype(BF16)
         c_ox(k).wait_recv()
         rb[k, 2:4] = (
@@ -428,13 +471,31 @@
         sums(k)
         c_ra(k).start()
         c_rk(k).start()
-        pair_back(k)
         return 0
 
     lax.fori_loop(1, 8, loop_sum, 0)
     sums(0)
     ret[s] = rb[0]
-    pair_back(0)
+    lax.fori_loop(0, 8, pair_back, 0)
+
+    def drain_in(k, _):
+        c_in_qa(k).wait_send()
+        c_in_kv(k).wait_send()
+        c_pa(k).wait_send()
+        return 0
+
+    lax.fori_loop(1, 8, drain_in, 0)
+
+    def drain_gather(k, _):
+        for d in (1, 3):
+            c_gy(k, d).wait_send()
+            c_gr(k, d).wait_send()
+        c_gx(k).wait_send()
+        c_gs(k).wait_send()
+        c_gf(k).wait_send()
+        return 0
+
+    lax.fori_loop(0, 8, drain_gather, 0)
 
     def wait_ret(k, _):
         c_ra(k).wait_recv()
@@ -458,6 +519,8 @@
         dpj[3, rows, :] = (gg[rows, :] * att * open_ * (1.0 - open_)).astype(BF16)
         for t in range(3):
             dpj[t, rows, :] = unshuffle(t + 1, q)
+    put_upd = pltpu.make_async_copy(upd, upd_out, lsem.at[14])
+    put_upd.start()
     for g in range(4):
         w = nn(nbt[...], dpj[g]).reshape(2, 8, 16, 256)
         ch[:, :, g * 16:(g + 1) * 16, :] = w
@@ -486,6 +549,34 @@
         mean_d = jnp.mean(d, axis=-1, keepdims=True)
         mean_x = jnp.mean(d * n, axis=-1, keepdims=True)
         alg[q] = (spread * (d - mean_d - n * mean_x)).astype(BF16)
+    put_alg = pltpu.make_async_copy(alg, alg_out, lsem.at[15])
+    put_alg.start()
+
+    def drain_out(k, _):
+        for d in (1, 3):
+            c_or(k, d).wait_send()
+            c_oy(k, d).wait_send()
+        c_os(k).wait_send()
+        c_ox(k).wait_send()
+        return 0
+
+    lax.fori_loop(0, 8, drain_out, 0)
+
+    def drain_ret(k, _):
+        c_ra(k).wait_send()
+        c_rk(k).wait_send()
+        c_da(k).wait_send()
+        return 0
+
+    lax.fori_loop(1, 8, drain_ret, 0)
+    for d in range(1, 4):
+        c_py(d).wait_send()
+        c_st(d).wait_send()
+        c_dy(d).wait_send()
+    for k in range(8):
+        store(k).wait()
+    put_upd.wait()
+    put_alg.wait()
     acc = ch2[s].astype(F32)
     for k in range(1, 8):
         c_ts(k).wait_recv()
@@ -515,40 +606,19 @@
     c_ac().start()
     c_ac().wait_recv()
 
+    put_sum = pltpu.make_async_copy(chf, chf_out, lsem.at[16])
+    put_sum.start()
+
     def drain(k, _):
-        c_in_qa(k).wait_send()
-        c_in_kv(k).wait_send()
-        c_pa(k).wait_send()
-        c_ra(k).wait_send()
-        c_rk(k).wait_send()
-        c_da(k).wait_send()
         c_ts(k).wait_send()
         c_as(k).wait_send()
         c_txy(k).wait_send()
         return 0
 
     lax.fori_loop(1, 8, drain, 0)
-    for k in range(8):
-        store(k).wait()
-
-    def drain_all(k, _):
-        for d in range(1, 4):
-            c_gy(k, d).wait_send()
-            c_oy(k, d).wait_send()
-        c_gx(k).wait_send()
-        c_gs(k).wait_send()
-        c_gf(k).wait_send()
-        c_os(k).wait_send()
-        c_ox(k).wait_send()
-        return 0
-
-    lax.fori_loop(0, 8, drain_all, 0)
-    for d in range(1, 4):
-        c_py(d).wait_send()
-        c_st(d).wait_send()
-        c_dy(d).wait_send()
     c_tc().wait_send()
     c_ac().wait_send()
+    put_sum.wait()
 
 
 def finish(upd_in, alg_in, pg_in, chf, upd, alg, pg, dcw, dow, dpw, tok, pair, isem, osem):
@@ -614,11 +684,19 @@
         V((96, 256), BF16),
         V((8, 96, 256), BF16),
         V((8, 128), F32),
+        V((8, 64, 256), BF16),
         V((64, 128, 128), BF16),
+        V((256, 1024), BF16),
+        V((256, 256), BF16),
+        V((8, 128), F32),
+        V((8, 64, 256), BF16),
+        V((8, 64, 256), BF16),
+        V((8, 64, 256), BF16),
         V((64, 128, 128), BF16),
+        V((2, 8, 96, 256), BF16),
         pltpu.SemaphoreType.DMA((SEM_COUNT,)),
         pltpu.SemaphoreType.DMA((SEM_COUNT,)),
-        pltpu.SemaphoreType.DMA((9,)),
+        pltpu.SemaphoreType.DMA((17,)),
     ]
     vm = pl.BlockSpec(memory_space=pltpu.VMEM)
     hbm = pl.BlockSpec(memory_space=pl.ANY)
@@ -627,8 +705,8 @@
     upd, alg, pg, chf = pl.pallas_call(
         kernel,
         out_shape=(tokens, tokens, pairs, jax.ShapeDtypeStruct((2, 8, 96, 256), BF16)),
-        in_specs=[vm, hbm, vm, vm, vm, vm],
-        out_specs=(vm, vm, hbm, vm),
+        in_specs=[hbm] * 6,
+        out_specs=(hbm,) * 4,
         scratch_shapes=scratch,
         compiler_params=pltpu.CompilerParams(
             collective_id=0, has_side_effects=True, vmem_limit_bytes=60 << 20

time: 118 us -> 114 us (0.966)
  Pallas kernels: 117 us -> 113 us
    pallas_call x1, Pallas kernels: 113 us -> 108 us  [body(): pl.pallas_call(kernel, out_shape=(tokens, tokens, pairs, jax.ShapeDtypeSt...]
where the time goes in v3:
time: 114 us
  Pallas kernels  113 us (99%)
    pallas_call x1, Pallas kernels, body(): pl.pallas_call(kernel, out_shape=(tokens, tokens, pairs, jax.ShapeDtypeSt...  108 us
    pallas_call x1, Pallas kernels, body(): pl.pallas_call(finish, out_shape=(tokens, tokens, pairs, jax.ShapeDtypeSt...  4.82 us

profile of v3, /device:TPU:1, one launch (start us, length us, event | category | flops | bytes accessed | tf_op | source)
XLA Modules:
  0.0 113.6 jit_solution(11511202238572870459)
XLA Ops:
  0.6 108.2 %row_attention.1 = (bf16[8,64,256]{2,1,0:T(8,128)(2,1)}, bf16[8,64,256]{2,1,0:T(8,128)(2,1)}, bf16[64,128,128]{2,1,0:T(8,128)(2,1)}, bf16[2,8,96,256]{3,2,1,0:T(8,128)(2,1)}) custom-call(bf16[8,64,256]{2,1,0:T(8,128)(2,1)} %al_in.1, bf16[64,128,128]{2,1,0:T(8,128)(2,1)} %pe_in.1, bf16[256,1024]{1,0:T(8,128)(2,1)} %cw_in.1, bf16[256,256]{1,0:T(8,128)(2,1)} %ow_in.1, ...), custom_call_target="tpu_custom_call" | custom-call | tf_op jit(solution)/shard_map/row_attention/pallas_call | solution.py:705
  108.8 4.8 %results.1 = (bf16[8,64,256]{2,1,0:T(8,128)(2,1)}, bf16[8,64,256]{2,1,0:T(8,128)(2,1)}, bf16[64,128,128]{2,1,0:T(8,128)(2,1)}, f32[256,1024]{1,0:T(8,128)}, f32[256,256]{1,0:T(8,128)}, /*index=5*/f32[8,128]{1,0:T(8,128)}) custom-call(bf16[8,64,256]{2,1,0:T(8,128)(2,1)} %get-tuple-element.16.upd_in, bf16[8,64,256]{2,1,0:T(8,128)(2,1)} %get-tuple-element.17.alg_in, ...), custom_call_target="tpu_custom_call" | custom-call | tf_op jit(solution)/shard_map/results/pallas_call | solution.py:716

commit v4 on v3

--- a/solution.py
+++ b/solution.py
@@ -19,7 +19,7 @@
 DL_Y, DL_A = 152, 156
 T_C, T_S, T_XY, T_AS, T_AC = 164, 165, 173, 181, 189
 SEM_COUNT = 190
-LAG = 2
+LAG = 3
 
 
 def nt(a, b):
@@ -213,8 +213,8 @@
     pl.semaphore_wait(bar, 15)
 
     def start_in(k, _):
+        c_in_kv(k).start()
         c_in_qa(k).start()
-        c_in_kv(k).start()
         return 0
 
     lax.fori_loop(1, 8, start_in, 0)
@@ -247,12 +247,12 @@
             bs[:, k * 8 + q, :] = b[:, q * 128:(q + 1) * 128]
 
     def stage_in(k, _):
+        c_in_kv(k).wait_recv()
+        c_gx(k).start()
+        c_gs(k).start()
         c_in_qa(k).wait_recv()
         for d in (1, 3):
             c_gy(k, d).start()
-        c_in_kv(k).wait_recv()
-        c_gx(k).start()
-        c_gs(k).start()
         pair_chunk(k)
         return 0
 
@@ -621,14 +621,20 @@
     put_sum.wait()
 
 
-def finish(upd_in, alg_in, pg_in, chf, upd, alg, pg, dcw, dow, dpw, tok, pair, isem, osem):
+def finish(
+    upd_in, alg_in, pg_in, chf_in, upd, alg, pg, dcw_out, dow_out, dpw_out,
+    tok, pair, chf, dcw, dow, dpw, isem, osem,
+):
     moves = [(pg_in.at[pl.ds(16 * a, 16)], pair.at[a], pg.at[pl.ds(16 * a, 16)]) for a in range(4)]
     moves.append((upd_in, tok.at[0], upd))
     moves.append((alg_in, tok.at[1], alg))
+    first = pltpu.make_async_copy(chf_in, chf, isem.at[6])
+    first.start()
     reads = [pltpu.make_async_copy(m[0], m[1], isem.at[i]) for i, m in enumerate(moves)]
     writes = [pltpu.make_async_copy(m[1], m[2], osem.at[i]) for i, m in enumerate(moves)]
     for copy in reads:
         copy.start()
+    first.wait()
     for b in range(2):
         for q in range(8):
             at = (b * 8 + q) * 16
@@ -636,10 +642,17 @@
                 dcw[at:at + 16, g * 256:(g + 1) * 256] = chf[b, q, g * 16:(g + 1) * 16, :].astype(F32)
             dow[at:at + 16, :] = chf[b, q, 64:80, :].astype(F32)
     dpw[...] = chf[0, 0, 80:96, 0:128].astype(F32)[0:8]
+    last = [
+        pltpu.make_async_copy(dcw, dcw_out, osem.at[6]),
+        pltpu.make_async_copy(dow, dow_out, osem.at[7]),
+        pltpu.make_async_copy(dpw, dpw_out, osem.at[8]),
+    ]
+    for copy in last:
+        copy.start()
     for read, write in zip(reads, writes):
         read.wait()
         write.start()
-    for copy in writes:
+    for copy in writes + last:
         copy.wait()
 
 
@@ -698,7 +711,6 @@
         pltpu.SemaphoreType.DMA((SEM_COUNT,)),
         pltpu.SemaphoreType.DMA((17,)),
     ]
-    vm = pl.BlockSpec(memory_space=pltpu.VMEM)
     hbm = pl.BlockSpec(memory_space=pl.ANY)
     tokens = jax.ShapeDtypeStruct((8, 64, 256), BF16)
     pairs = jax.ShapeDtypeStruct((64, 128, 128), BF16)
@@ -723,13 +735,17 @@
             jax.ShapeDtypeStruct((256, 256), F32),
             jax.ShapeDtypeStruct((8, 128), F32),
         ),
-        in_specs=[hbm, hbm, hbm, vm],
-        out_specs=(hbm, hbm, hbm, vm, vm, vm),
+        in_specs=[hbm] * 4,
+        out_specs=(hbm,) * 6,
         scratch_shapes=[
             V((2, 8, 64, 256), BF16),
             V((4, 16, 128, 128), BF16),
-            pltpu.SemaphoreType.DMA((6,)),
-            pltpu.SemaphoreType.DMA((6,)),
+            V((2, 8, 96, 256), BF16),
+            V((256, 1024), F32),
+            V((256, 256), F32),
+            V((8, 128), F32),
+            pltpu.SemaphoreType.DMA((7,)),
+            pltpu.SemaphoreType.DMA((9,)),
         ],
         compiler_params=pltpu.CompilerParams(vmem_limit_bytes=60 << 20),
         name="results",

time: 114 us -> 111 us (0.974)
  Pallas kernels: 113 us -> 111 us
    pallas_call x1, Pallas kernels: 4.82 us -> 3.26 us  [body(): pl.pallas_call(finish, out_shape=(tokens, tokens, pairs, jax.ShapeDtypeSt...]
where the time goes in v4:
time: 111 us
  Pallas kernels  111 us (100%)
    pallas_call x1, Pallas kernels, body(): pl.pallas_call(kernel, out_shape=(tokens, tokens, pairs, jax.ShapeDtypeSt...  107 us
    pallas_call x1, Pallas kernels, body(): pl.pallas_call(finish, out_shape=(tokens, tokens, pairs, jax.ShapeDtypeSt...  3.26 us

profile of v4, /device:TPU:1, one launch (start us, length us, event | category | flops | bytes accessed | tf_op | source)
XLA Modules:
  0.0 111.2 jit_solution(16319271772744574200)
XLA Ops:
  0.6 107.3 %row_attention.1 = (bf16[8,64,256]{2,1,0:T(8,128)(2,1)}, bf16[8,64,256]{2,1,0:T(8,128)(2,1)}, bf16[64,128,128]{2,1,0:T(8,128)(2,1)}, bf16[2,8,96,256]{3,2,1,0:T(8,128)(2,1)}) custom-call(bf16[8,64,256]{2,1,0:T(8,128)(2,1)} %al_in.1, bf16[64,128,128]{2,1,0:T(8,128)(2,1)} %pe_in.1, bf16[256,1024]{1,0:T(8,128)(2,1)} %cw_in.1, bf16[256,256]{1,0:T(8,128)(2,1)} %ow_in.1, ...), custom_call_target="tpu_custom_call" | custom-call | tf_op jit(solution)/shard_map/row_attention/pallas_call | solution.py:717
  108.0 3.3 %results.1 = (bf16[8,64,256]{2,1,0:T(8,128)(2,1)}, bf16[8,64,256]{2,1,0:T(8,128)(2,1)}, bf16[64,128,128]{2,1,0:T(8,128)(2,1)}, f32[256,1024]{1,0:T(8,128)}, f32[256,256]{1,0:T(8,128)}, /*index=5*/f32[8,128]{1,0:T(8,128)}) custom-call(bf16[8,64,256]{2,1,0:T(8,128)(2,1)} %get-tuple-element.16.upd_in, bf16[8,64,256]{2,1,0:T(8,128)(2,1)} %get-tuple-element.17.alg_in, ...), custom_call_target="tpu_custom_call" | custom-call | tf_op jit(solution)/shard_map/results/pallas_call | solution.py:728

commit v5 on v4

--- a/solution.py
+++ b/solution.py
@@ -353,10 +353,6 @@
         dak = qa[k, :, 1].reshape(256, 256)
         kk = kv[k, :, 0].reshape(256, 256)
         vk = kv[k, :, 1].reshape(256, 256)
-        oa[k, :, 0] = nn(bt[1], vk).astype(BF16).reshape(4, 64, 256)
-        oa[k, :, 1] = (nn(bt[3], kk) * SCALE).astype(BF16).reshape(4, 64, 256)
-        for d in (1, 3):
-            c_or(k, d).start()
         dk = nn(bt[2], qk).astype(BF16)
         dv = nn(bt[0], dak).astype(BF16)
         for a in range(2):
@@ -365,6 +361,10 @@
                 okv[k, b, a, 0] = dk[at:at + 64]
                 okv[k, b, a, 1] = dv[at:at + 64]
         c_os(k).start()
+        oa[k, :, 0] = nn(bt[1], vk).astype(BF16).reshape(4, 64, 256)
+        oa[k, :, 1] = (nn(bt[3], kk) * SCALE).astype(BF16).reshape(4, 64, 256)
+        for d in (1, 3):
+            c_or(k, d).start()
 
     def stage_y(k):
         for d in (1, 3):

time: 111 us -> 111 us (level)
  no operation moved by 1% of the time
where the time goes in v5:
time: 111 us
  Pallas kernels  110 us (99%)
    pallas_call x1, Pallas kernels, body(): pl.pallas_call(kernel, out_shape=(tokens, tokens, pairs, jax.ShapeDtypeSt...  107 us
    pallas_call x1, Pallas kernels, body(): pl.pallas_call(finish, out_shape=(tokens, tokens, pairs, jax.ShapeDtypeSt...  3.26 us

profile of v5, /device:TPU:1, one launch (start us, length us, event | category | flops | bytes accessed | tf_op | source)
XLA Modules:
  0.0 111.1 jit_solution(10177736949217935876)
XLA Ops:
  0.6 107.2 %row_attention.1 = (bf16[8,64,256]{2,1,0:T(8,128)(2,1)}, bf16[8,64,256]{2,1,0:T(8,128)(2,1)}, bf16[64,128,128]{2,1,0:T(8,128)(2,1)}, bf16[2,8,96,256]{3,2,1,0:T(8,128)(2,1)}) custom-call(bf16[8,64,256]{2,1,0:T(8,128)(2,1)} %al_in.1, bf16[64,128,128]{2,1,0:T(8,128)(2,1)} %pe_in.1, bf16[256,1024]{1,0:T(8,128)(2,1)} %cw_in.1, bf16[256,256]{1,0:T(8,128)(2,1)} %ow_in.1, ...), custom_call_target="tpu_custom_call" | custom-call | tf_op jit(solution)/shard_map/row_attention/pallas_call | solution.py:717
  107.8 3.3 %results.1 = (bf16[8,64,256]{2,1,0:T(8,128)(2,1)}, bf16[8,64,256]{2,1,0:T(8,128)(2,1)}, bf16[64,128,128]{2,1,0:T(8,128)(2,1)}, f32[256,1024]{1,0:T(8,128)}, f32[256,256]{1,0:T(8,128)}, /*index=5*/f32[8,128]{1,0:T(8,128)}) custom-call(bf16[8,64,256]{2,1,0:T(8,128)(2,1)} %get-tuple-element.16.upd_in, bf16[8,64,256]{2,1,0:T(8,128)(2,1)} %get-tuple-element.17.alg_in, ...), custom_call_target="tpu_custom_call" | custom-call | tf_op jit(solution)/shard_map/results/pallas_call | solution.py:728
